TPU v7x, 256 devices: a whole 4x4x8 slice. The times are simulated.
256 devices in a mesh: section: 8 (over x, y_lo), expert: 32 (over z, y_hi, core).
Axes of the slice: x: 4, y: 4 (y_hi: 2, y_lo: 2; y = y_hi * 2 + y_lo), z: 8, core: 2. Of those that a mesh axis runs over, the one named last changes fastest.
Arguments:
- act_up: bfloat16 [8, 4096, 3584], P('section', 'expert'), may hold values from -6 to 6
- routes_up: int32 [8, 4096, 1], P('section', 'expert'), may hold values from 0 to 7; in each aligned block of 128 rows (0 to 127, 128 to 255, ..., all dimensions but the last counted through in order) at most 24 rows name the same one
- gates_up: float32 [8, 4096, 1], P('section', 'expert'), may hold values from 0.3 to 1
- saved_down: bfloat16 [8, 4096, 3584], P('section', 'expert'), may hold values from -6 to 6
- grad_down: bfloat16 [8, 4096, 3584], P('section', 'expert'), may hold values from -4 to 4
- routes_down: int32 [8, 4096, 1], P('section', 'expert'), may hold values from 0 to 7; in each aligned block of 128 rows (0 to 127, 128 to 255, ..., all dimensions but the last counted through in order) at most 24 rows name the same one
- gates_down: float32 [8, 4096, 1], P('section', 'expert'), may hold values from 0.3 to 1
- norm_gain: float32 [8, 3584], P('section'), may hold values from 0.1 to 1.9
- w_gate: bfloat16 [8, 32, 3584, 256], P('section', 'expert'), may hold values from -0.09375 to 0.09375
- w_up: bfloat16 [8, 32, 3584, 256], P('section', 'expert'), may hold values from -0.09375 to 0.09375
- w_down: bfloat16 [8, 32, 256, 3584], P('section', 'expert'), may hold values from -0.1875 to 0.1875
Outputs:
- arriving_up: bfloat16 [8, 4096, 3584], P('section', 'expert')
- arriving_down: bfloat16 [8, 4096, 3584], P('section', 'expert')
Inputs may be any that keep to these rules, and one draw needn't show every extreme that they name: `routes_up`: among the 128 tokens of one device at one section, no expert is named more than 24 times, a bound that some block reaches; a token names 1 different experts. `routes_down`: among the 128 tokens of one device at one section, no expert is named more than 24 times, a bound that some block reaches; a token names 1 different experts.
All inputs are finite; a program needn't handle non-finite values.
Results may differ from a plain program's by a relative error of at most 0.0059.
Values may be sent and summed in bfloat16 or wider, within the bound.
A program may use at most 128 MiB of HBM per device.

v0:
```python
import jax
import jax.numpy as jnp
from jax import lax
from jax.sharding import PartitionSpec as P

SLICES = 4


EPS = 1e-06


def shifted(array, axis, by):
    size = lax.axis_size(axis)
    return lax.ppermute(array, axis, [(i, (i + by) % size) for i in range(size)])


def normalize(inputs, gain_row):
    values = inputs.astype(jnp.float32)
    scaling = lax.rsqrt(jnp.mean(values * values, axis=-1, keepdims=True) + EPS)
    return (values, scaling, (values * scaling * gain_row).astype(jnp.bfloat16))


def slot_positions(routes, experts, capacity):
    entries = routes.reshape(-1)
    onehot = (entries[:, None] == jnp.arange(experts, dtype=jnp.int32)[None, :]).astype(jnp.int32)
    before = jnp.cumsum(onehot, axis=0) - onehot
    return entries * capacity + jnp.sum(before * onehot, axis=1)


def pack_rows(positions, table, slot_total):
    select = (jnp.arange(slot_total, dtype=jnp.int32)[:, None] == positions[None, :]).astype(
        table.dtype
    )
    return jnp.dot(select, table, preferred_element_type=jnp.float32).astype(table.dtype)


def contract_last(matrix, weights):
    return lax.dot_general(
        matrix, weights, (((1,), (1,)), ((), ())), preferred_element_type=jnp.float32
    )


def expert_rows(stacked, features, gate_mat, up_mat, down_mat):
    normed_up = stacked[:, :features]
    normed_down = stacked[:, features : 2 * features]
    grad_rows = stacked[:, 2 * features :]
    gate_act = jnp.dot(normed_up, gate_mat, preferred_element_type=jnp.float32)
    up_act = jnp.dot(normed_up, up_mat, preferred_element_type=jnp.float32)
    middle = (jax.nn.silu(gate_act) * up_act).astype(jnp.bfloat16)
    forward_part = jnp.dot(middle, down_mat, preferred_element_type=jnp.float32).astype(
        jnp.bfloat16
    )
    gate_back = jnp.dot(normed_down, gate_mat, preferred_element_type=jnp.float32)
    up_back = jnp.dot(normed_down, up_mat, preferred_element_type=jnp.float32)
    pulled = contract_last(grad_rows, down_mat)
    sigma_gate = jax.nn.sigmoid(gate_back)
    silu_gate = gate_back * sigma_gate
    d_gate = (pulled * up_back * sigma_gate * (1.0 + gate_back * (1.0 - sigma_gate))).astype(
        jnp.bfloat16
    )
    d_upper = (pulled * silu_gate).astype(jnp.bfloat16)
    backward_part = (contract_last(d_gate, gate_mat) + contract_last(d_upper, up_mat)).astype(
        jnp.bfloat16
    )
    return jnp.concatenate([forward_part, backward_part], axis=1)


def per_device(
    act_up,
    routes_up,
    gates_up,
    saved_down,
    grad_down,
    routes_down,
    gates_down,
    norm_gain,
    w_gate,
    w_up,
    w_down,
):
    tok_count = act_up.shape[1]
    features = act_up.shape[2]
    top_count = routes_up.shape[2]
    groups = lax.axis_size("expert")
    experts = groups // SLICES
    capacity = SLICES * (
        (3 * tok_count * top_count + 2 * experts * SLICES - 1) // (2 * experts * SLICES)
    )
    slot_total = experts * capacity
    gain_row = norm_gain[0]
    gate_local = w_gate[0, 0]
    up_local = w_up[0, 0]
    down_local = w_down[0, 0]
    values_up, scaling_up, normed_up = normalize(act_up[0], gain_row)
    values_down, scaling_down, normed_down = normalize(saved_down[0], gain_row)
    places_up = slot_positions(routes_up[0], experts, capacity)
    places_down = slot_positions(routes_down[0], experts, capacity)
    packed_up = pack_rows(places_up, jnp.repeat(normed_up, top_count, axis=0), slot_total)
    table_down = jnp.concatenate(
        [jnp.repeat(normed_down, top_count, axis=0), jnp.repeat(grad_down[0], top_count, axis=0)],
        axis=1,
    )
    packed_down = pack_rows(places_down, table_down, slot_total)
    outgoing = jnp.concatenate([packed_up, packed_down], axis=1).reshape(
        experts, capacity, 3 * features
    )
    pieces = lax.all_to_all(
        jnp.tile(outgoing, (SLICES, 1, 1)), "expert", split_axis=0, concat_axis=0, tiled=True
    )
    item_count = pieces.shape[1]
    computed = expert_rows(
        pieces.reshape(-1, 3 * features), features, gate_local, up_local, down_local
    )
    returned_rows = lax.all_to_all(
        computed.reshape(groups, item_count, 2 * features),
        "expert",
        split_axis=0,
        concat_axis=0,
        tiled=True,
    )
    summed = jnp.sum(
        returned_rows.astype(jnp.float32).reshape(SLICES, slot_total, 2 * features), axis=0
    )
    back_up = jnp.take(summed[:, :features], places_up, axis=0).reshape(
        tok_count, top_count, features
    )
    back_down = jnp.take(summed[:, features:], places_down, axis=0).reshape(
        tok_count, top_count, features
    )
    mixed_up = jnp.sum(back_up * gates_up[0][:, :, None], axis=1)
    layer_up = (values_up + mixed_up).astype(jnp.bfloat16)
    pulled_in = jnp.sum(back_down * gates_down[0][:, :, None], axis=1) * gain_row
    cubed = scaling_down * scaling_down * scaling_down
    result = grad_down[0].astype(jnp.float32) + scaling_down * pulled_in
    result = result - values_down * cubed * jnp.mean(
        values_down * pulled_in, axis=-1, keepdims=True
    )
    layer_down = result.astype(jnp.bfloat16)
    arriving_up = shifted(layer_up[None], "section", 1)
    arriving_down = shifted(layer_down[None], "section", -1)
    return (arriving_up, arriving_down)


def solution(mesh):
    in_specs = (
        P("section", "expert", None),
        P("section", "expert", None),
        P("section", "expert", None),
        P("section", "expert", None),
        P("section", "expert", None),
        P("section", "expert", None),
        P("section", "expert", None),
        P("section", None),
        P("section", "expert", None, None),
        P("section", "expert", None, None),
        P("section", "expert", None, None),
    )
    out_specs = (P("section", "expert", None), P("section", "expert", None))
    return jax.shard_map(
        per_device, mesh=mesh, in_specs=in_specs, out_specs=out_specs, check_vma=False
    )
```

profile of v0, /device:TPU:25, one launch (start us, length us, event | category | flops | bytes accessed | tf_op | source)
XLA Modules:
  0.0 751.0 jit_solution(15875999395742784474)
XLA Ops:
  0.6 0.0 copy-start
  0.6 0.0 copy-start.4
  0.7 0.0 copy-start.9
  0.7 1.6 fusion.19
  2.3 0.7 fusion.91
  3.0 0.2 reduce_window_sum.18
  3.2 0.8 select_reduce_fusion
  4.0 0.7 compare_and_fusion
  4.7 0.7 fusion.92
  5.4 0.2 reduce_window_sum.17
  5.6 0.8 select_reduce_fusion.1
  6.5 0.7 compare_and_fusion.1
  7.1 1.4 fusion.15
  8.6 0.0 copy-start.6
  8.7 0.0 copy-start.7
  8.7 0.3 fusion.21
  8.9 0.9 copy-done.6
  9.8 0.6 convolution_convert_fusion.2
  10.4 0.9 convolution_convert_fusion
  11.3 0.3 pad_maximum_fusion.1
  11.6 1.2 tile.11
  12.8 0.0 copy-start.8
  12.8 371.7 %all_to_all.10 = bf16[32,24,10752]{2,1,0:T(8,128)(2,1)S(1)} all-to-all(bf16[32,24,10752]{2,1,0:T(8,128)(2,1)S(1)} %bitcast.87), channel_id=1, replica_groups=mesh['section'=8,'expert'=32] {'expert'}, dimensions={0} | all-to-all | bytes 33030144 | tf_op jit(solution)/shard_map/all_to_all | solution.py:107
  384.5 1.6 fusion.2
  386.1 0.0 copy-start.12
  386.1 2.5 fusion.8
  388.6 2.3 copy-done.2
  390.9 1.6 fusion
  392.5 13.1 %fusion.34 = f32[768,3584]{1,0:T(8,128)} fusion(bf16[1,1,3584,256]{3,2,1,0:T(8,128)(2,1)} %param.21, f32[768,256]{1,0:T(8,128)S(1)} %fusion, bf16[1,1,3584,256]{3,2,1,0:T(8,128)(2,1)S(1)} %copy-done, bf16[768,10752]{1,0:T(8,128)(2,1)} %bitcast.92, f32[768,256]{1,0:T(8,128)S(1)} %fusion.2), kind=kOutput, calls=%fused_computation.48 | convolution fusion | flops 2820538368 | bytes 21757952 | tf_op jit(solution)/shard_map/dot_general | solution.py:38
  405.6 8.2 %add_convert_fusion = bf16[768,3584]{1,0:T(8,128)(2,1)} fusion(f32[768,3584]{1,0:T(8,128)} %fusion.34, bf16[1,1,3584,256]{3,2,1,0:T(8,128)(2,1)S(1)} %copy-done, f32[768,256]{1,0:T(8,128)S(1)} %fusion, f32[768,256]{1,0:T(8,128)S(1)} %fusion.2), kind=kOutput, calls=%fused_computation.4 | convolution fusion | flops 1415970816 | bytes 19922944 | tf_op jit(solution)/shard_map/dot_general | solution.py:38
  413.8 11.5 %convolution_convert_fusion.1 = bf16[768,3584]{1,0:T(8,128)(2,1)} fusion(bf16[1,1,256,3584]{3,2,1,0:T(8,128)(2,1)} %param.23, bf16[1,1,3584,256]{3,2,1,0:T(8,128)(2,1)S(1)} %copy-done, bf16[768,10752]{1,0:T(8,128)(2,1)} %bitcast.93, f32[768,256]{1,0:T(8,128)} %fusion.8), kind=kOutput, calls=%fused_computation.6 | convolution fusion | flops 2822504448 | bytes 15466496 | tf_op jit(solution)/shard_map/dot_general | solution.py:50
  425.3 9.6 %pad_maximum_fusion = bf16[768,7168]{1,0:T(8,128)(2,1)} fusion(bf16[768,3584]{1,0:T(8,128)(2,1)} %add_convert_fusion, bf16[768,3584]{1,0:T(8,128)(2,1)} %convolution_convert_fusion.1), kind=kLoop, calls=%fused_computation.3 | loop fusion | flops 22020096 | bytes 22020096 | tf_op jit(solution)/shard_map/concatenate | solution.py:65
  434.9 5.5 all-to-all-start.1
  440.5 240.2 %all-to-all-done.1 = bf16[32,24,7168]{2,1,0:T(8,128)(2,1)} async-done(((bf16[32,24,7168]{2,1,0:T(8,128)(2,1)}), bf16[32,24,7168]{2,1,0:T(8,128)(2,1)}, u32[]{:S(2)}, u32[]{:S(2)}) %all-to-all-start.1) | async-done | bytes 11010080 | tf_op jit(solution)/shard_map/all_to_all | solution.py:114
  680.7 9.1 %convert_reduce_fusion = f32[192,7168]{1,0:T(8,128)} fusion(bf16[4,192,7168]{2,1,0:T(8,128)(2,1)} %bitcast.86), kind=kLoop, calls=%fused_computation.2 | loop fusion | flops 9633792 | bytes 16515072 | tf_op jit(solution)/shard_map/reduce_sum | solution.py:121
  689.8 4.5 fusion.99
  694.3 5.0 gather_fusion.1
  699.3 2.4 fusion.22
  701.7 0.1 copy-done.5
  701.8 3.0 fusion.25
  704.9 0.4 collective-permute-start.1
  705.3 2.4 gather_fusion
  707.7 2.3 fusion.18
  710.0 2.0 collective-permute-start
  712.0 32.5 %collective-permute-done.1 = bf16[1,128,3584]{2,1,0:T(8,128)(2,1)} collective-permute-done((bf16[1,128,3584]{2,1,0:T(8,128)(2,1)}, bf16[1,128,3584]{2,1,0:T(8,128)(2,1)}, u32[]{:S(2)}, u32[]{:S(2)}) %collective-permute-start.1) | collective-permute-done | bytes 917536 | tf_op jit(solution)/shard_map/ppermute | solution.py:14
  744.5 3.4 collective-permute-done
  747.9 0.9 copy.15
  748.8 2.2 copy.16
  (24 shorter events, 0.1 us)
Async XLA Ops:
  0.6 391.9 %copy-start = (bf16[1,1,3584,256]{3,2,1,0:T(8,128)(2,1)S(1)}, bf16[1,1,3584,256]{3,2,1,0:T(8,128)(2,1)}, u32[]{:S(2)}) copy-start(bf16[1,1,3584,256]{3,2,1,0:T(8,128)(2,1)} %param.22) | copy-start | bytes 5505028
  0.6 8.0 %copy-start.4 = (bf16[1,128,3584]{2,1,0:T(8,128)(2,1)S(1)}, bf16[1,128,3584]{2,1,0:T(8,128)(2,1)}, u32[]{:S(2)}) copy-start(bf16[1,128,3584]{2,1,0:T(8,128)(2,1)} %param.16) | copy-start | bytes 2752516
  0.7 7.9 %copy-start.9 = (f32[1,3584]{1,0:T(1,128)S(1)}, f32[1,3584]{1,0:T(1,128)}, u32[]{:S(2)}) copy-start(f32[1,3584]{1,0:T(1,128)} %param.20) | copy-start | bytes 43012
  8.6 1.2 copy-start.6
  8.7 1.8 copy-start.7
  12.8 371.7 %copy-start.8 = (bf16[1,1,3584,256]{3,2,1,0:T(8,128)(2,1)S(1)}, bf16[1,1,3584,256]{3,2,1,0:T(8,128)(2,1)}, u32[]{:S(2)}) copy-start(bf16[1,1,3584,256]{3,2,1,0:T(8,128)(2,1)} %param.21) | copy-start | bytes 5505028
  384.5 6.4 copy-start.2
  386.1 4.8 copy-start.12
  434.9 245.8 %all-to-all-start.1 = ((bf16[32,24,7168]{2,1,0:T(8,128)(2,1)}), bf16[32,24,7168]{2,1,0:T(8,128)(2,1)}, u32[]{:S(2)}, u32[]{:S(2)}) async-start(bf16[32,24,7168]{2,1,0:T(8,128)(2,1)} %bitcast.88), calls=%async_computation.1 | async-start | bytes 22020096 | tf_op jit(solution)/shard_map/all_to_all | solution.py:114
  694.3 5.0 copy-start.10
  699.3 2.5 copy-start.3
  699.3 2.6 copy-start.5
  704.9 39.7 %collective-permute-start.1 = (bf16[1,128,3584]{2,1,0:T(8,128)(2,1)}, bf16[1,128,3584]{2,1,0:T(8,128)(2,1)}, u32[]{:S(2)}, u32[]{:S(2)}) collective-permute-start(bf16[1,128,3584]{2,1,0:T(8,128)(2,1)} %fusion.25), channel_id=1, source_target_pairs={{0,224},{32,0},{64,32},{96,64},{128,96},{160,128},{192,160},{224,1... | collective-permute-start | bytes 2752520 | tf_op jit(solution)/shard_map/ppermute | solution.py:14
  705.3 2.4 copy-start.11
  707.7 43.3 %copy-start.1 = (bf16[1,1,3584,256]{3,2,1,0:T(8,128)(2,1)S(1)}, bf16[1,1,3584,256]{3,2,1,0:T(8,128)(2,1)}, u32[]{:S(2)}) copy-start(bf16[1,1,3584,256]{3,2,1,0:T(8,128)(2,1)} %param.22) | copy-start | bytes 5505028
  710.0 37.9 %collective-permute-start = (bf16[1,128,3584]{2,1,0:T(8,128)(2,1)S(1)}, bf16[1,128,3584]{2,1,0:T(8,128)(2,1)S(1)}, u32[]{:S(2)}, u32[]{:S(2)}) collective-permute-start(bf16[1,128,3584]{2,1,0:T(8,128)(2,1)S(1)} %fusion.18), channel_id=1, source_target_pairs={{0,32},{32,64},{64,96},{96,128},{128,160},{160,192},{192,224},{224... | collective-permute-start | bytes 2752520 | tf_op jit(solution)/shard_map/ppermute | solution.py:14
where the time goes:
time: 755 us; the launch traced here: 751 us
  blocking collectives  372 us (49%)
  waiting for transfers between devices  276 us (37%)
  matrix products  39.9 us (5%)
  other arithmetic  34.9 us (5%)
  local copies, waits for them, and re-layouts  19.5 us (3%)
  starting transfers between devices  7.98 us (1%)
    all_to_all x1, blocking collectives, per_device(): lax.all_to_all(jnp.tile(outgoing, (SLICES, 1, 1)), 'expert', split_axis=0...  372 us
    all_to_all x1, waiting for transfers between devices, per_device(): lax.all_to_all(computed.reshape(groups, item_count, 2 * features), 'exper...  240 us
    ppermute x2, waiting for transfers between devices, shifted(): lax.ppermute(array, axis, [(i, (i + by) % size) for i in range(size)])  35.9 us
    dot_general x3, matrix products, contract_last(): lax.dot_general(matrix, weights, (((1,), (1,)), ((), ())), preferred_elem...  22.9 us
  transfers between devices with their start and end apart: 3, of which 3 were waited for; matrix products, arithmetic and copies ran while one was open for 1% of the time, Pallas kernels for 0%

commit v1 on v0

v1 whole, which is shorter than its diff:
```python
import functools

import jax
import jax.numpy as jnp
from jax import lax
from jax.experimental import pallas as pl
from jax.experimental.pallas import tpu as pltpu
from jax.sharding import PartitionSpec as P

EPS = 1e-06
CAP = 24
BLOCK = 2 * CAP
EXPERTS = 8
SLICES = 4
MIB = 1024 * 1024
MESH = pl.DeviceIdType.MESH
F32 = jnp.float32
BF16 = jnp.bfloat16


def nearest(rel):
    inside = lax.rem(rel + 7, 8) // 4
    second = 1 - inside
    dist = second * (rel - 1) + inside * lax.rem(8 - rel, 8)
    return second, dist


def expert_home(zl, yh, c):
    return zl * 4 + yh * 2 + c


def column(row):
    n = row.shape[1]
    eye = lax.broadcasted_iota(jnp.int32, (n, n), 0) == lax.broadcasted_iota(jnp.int32, (n, n), 1)
    return jnp.sum(jnp.where(eye, row, 0.0), axis=1, keepdims=True)


def block_rows(route_row):
    n = route_row.shape[1]
    earlier = lax.broadcasted_iota(jnp.int32, (n, n), 0) < lax.broadcasted_iota(jnp.int32, (n, n), 1)
    same = jnp.logical_and(column(route_row) == route_row, earlier)
    slot = jnp.sum(jnp.where(same, 1.0, 0.0), axis=0, keepdims=True)
    return route_row * float(BLOCK) + slot


def contract_last(a, b):
    return lax.dot_general(a, b, (((1,), (1,)), ((), ())), preferred_element_type=F32)


def kernel(
    act, saved, grad, gain, meta, wg_in, wu_in, wd_in,
    out_up, out_dn,
    wg, wu, wd, table, packed, rows_in, acc_up, acc_dn,
    back_up_out, back_dn_out, back_up_in, back_dn_in,
    act_in, saved_in, grad_in, gain_in, meta_up_in, meta_dn_in,
    row_send, row_recv, src_send, w_recv, sib_send, fwd_send,
    up_send, up_recv, dn_send, dn_recv, res_send, res_recv,
):
    tokens, features = act.shape
    half = features // 2
    hidden = wg_in.shape[1]
    n_sec = lax.axis_size("section")
    sec = lax.axis_index("section")
    me = lax.axis_index("expert")
    z, yh, c = me // 4, lax.rem(me // 2, 2), lax.rem(me, 2)
    after = lax.rem(sec + 1, n_sec)
    before = lax.rem(sec + n_sec - 1, n_sec)

    own_zl = lax.rem(z, 2)
    own_first = 2 * (2 * c + own_zl)
    own_rel = lax.rem(z - own_first + 8, 8)
    own_second, _ = nearest(own_rel)
    own_host = own_first + own_second
    m = own_rel // 2
    own_place = (1 - own_zl) * (m + m // 2 - 2 * (m // 3)) + own_zl * (2 * m - m // 2 - 4 * (m // 3))

    pair = z // 2
    side = lax.rem(z, 2)
    host_zl, host_c = lax.rem(pair, 2), pair // 2
    host_expert = expert_home(host_zl, yh, host_c)
    other_host = (2 * pair + 1 - side) * 4 + yh * 2 + c
    sibling = z * 4 + yh * 2 + 1 - c
    leads_even = 1 - lax.rem(host_zl + side, 2)

    def source(dist, src_yh):
        src_z = lax.rem(2 * pair + side + (2 * side - 1) * dist + 8, 8)
        return src_z * 4 + src_yh * 2 + c

    def host_of(g):
        zl, g_yh, g_c = g // 4, (g // 2) % 2, g % 2
        first = 2 * (2 * g_c + zl)
        second, dist = nearest(lax.rem(z - first + 8, 8))
        return (first + second) * 4 + g_yh * 2 + c, dist * 2 + yh

    def slice_source(place):
        rel = (1 - host_zl) * (0, 2, 6, 4)[place] + host_zl * (1, 7, 3, 5)[place]
        return lax.rem(2 * pair + rel, 8) * 4 + yh * 2 + host_c

    barrier = pltpu.get_barrier_semaphore()

    def greet(section, peer):
        pl.semaphore_signal(barrier, inc=1, device_id=(section, peer), device_id_type=MESH)

    for dist in range(4):
        for src_yh in range(2):
            peer = source(dist, src_yh)

            @pl.when(peer != me)
            def _():
                greet(sec, peer)

    for place in range(4):
        peer = slice_source(place)
        leads = leads_even if place % 2 == 0 else 1 - leads_even

        @pl.when(jnp.logical_and(leads == 1, peer != me))
        def _():
            greet(sec, peer)

    greet(sec, other_host)
    greet(sec, sibling)
    for g in range(EXPERTS):
        peer, _ = host_of(g)
        greet(before, peer)
        greet(after, peer)
    greet(before, me)
    greet(after, me)
    here = jnp.where(own_host == z, 1, 0)
    pl.semaphore_wait(barrier, 29 - here)

    mats = ((wg_in, wg), (wu_in, wu), (wd_in, wd))

    def w_half(ref, index, h):
        size = mats[index][0].shape[0] // 2
        return ref.at[pl.ds(pl.multiple_of(h * size, 128), size)]

    def remote(src, dst, send, recv, section, peer):
        return pltpu.make_async_remote_copy(
            src_ref=src, dst_ref=dst, send_sem=send, recv_sem=recv,
            device_id=(section, peer), device_id_type=MESH,
        )

    def slice_copy(index, h):
        src, dst = mats[index]
        return remote(
            w_half(src, index, h), w_half(dst.at[own_place], index, h),
            src_send.at[index, h], w_recv.at[own_place, index, h], sec, own_host * 4 + yh * 2 + h,
        )

    for index in range(3):
        for h in range(2):
            mine = jnp.logical_and(own_host == z, c == h)

            @pl.when(mine)
            def _():
                src, dst = mats[index]
                pltpu.make_async_copy(
                    w_half(src, index, h), w_half(dst.at[own_place], index, h), w_recv.at[own_place, index, h]
                ).start()

            @pl.when(jnp.logical_not(mine))
            def _():
                slice_copy(index, h).start()

    gain_row = gain[...]
    rows_step = 16

    def norm_rows(step, _):
        at = pl.ds(pl.multiple_of(step * rows_step, rows_step), rows_step)
        for source_ref, base in ((act, 0), (saved, tokens)):
            values = source_ref[at, :].astype(F32)
            scaling = lax.rsqrt(jnp.mean(values * values, axis=-1, keepdims=True) + EPS)
            to = pl.ds(pl.multiple_of(base + step * rows_step, rows_step), rows_step)
            table[to, :features] = (values * scaling * gain_row).astype(BF16)
        return 0

    lax.fori_loop(0, tokens // rows_step, norm_rows, 0)
    table[:tokens, features:] = grad[:, :half]
    table[tokens:, features:] = grad[:, half:]

    at_up = block_rows(meta[0:1, :])
    at_dn = block_rows(meta[2:3, :])
    n_rows = EXPERTS * BLOCK
    row_index = lax.broadcasted_iota(jnp.int32, (n_rows, 2 * tokens), 0).astype(F32)
    pick_h = (row_index == jnp.concatenate([at_up, at_dn + float(CAP)], axis=1)).astype(BF16)
    pick_g = (row_index == jnp.concatenate([at_dn, at_dn + float(CAP)], axis=1)).astype(BF16)
    width = 256

    def pack(first, pick):
        def body(step, _):
            at = pl.ds(pl.multiple_of(first + step * width, width), width)
            packed[:, at] = jnp.dot(pick, table[:, at], preferred_element_type=F32).astype(BF16)
            return 0

        return body

    lax.fori_loop(0, features // width, pack(0, pick_h), 0)
    lax.fori_loop(0, half // width, pack(features, pick_g), 0)

    def row_block(ref, index):
        return ref.at[pl.ds(pl.multiple_of(index * BLOCK, BLOCK), BLOCK)]

    def row_copy(g):
        peer, slot = host_of(g)
        return peer, remote(
            row_block(packed, g), row_block(rows_in, slot), row_send.at[g], row_recv.at[slot], sec, peer
        )

    for g in range(EXPERTS):
        peer, slot = host_of(g)

        @pl.when(peer == me)
        def _():
            pltpu.make_async_copy(row_block(packed, g), row_block(rows_in, slot), row_recv.at[slot]).start()

        @pl.when(peer != me)
        def _():
            row_copy(g)[1].start()

    residuals = [
        remote(act, act_in, res_send.at[0], res_recv.at[0], after, me),
        remote(meta, meta_up_in, res_send.at[1], res_recv.at[1], after, me),
        remote(saved, saved_in, res_send.at[2], res_recv.at[2], before, me),
        remote(grad, grad_in, res_send.at[3], res_recv.at[3], before, me),
        remote(gain, gain_in, res_send.at[4], res_recv.at[4], before, me),
        remote(meta, meta_dn_in, res_send.at[5], res_recv.at[5], before, me),
    ]
    for copy in residuals:
        copy.start()

    acc_up[...] = jnp.zeros_like(acc_up)
    acc_dn[...] = jnp.zeros_like(acc_dn)

    def half_copy(place, index, h, send, peer):
        view = w_half(mats[index][1].at[place], index, h)
        return remote(view, view, send, w_recv.at[place, index, h], sec, peer)

    def sibling_copy(place, index):
        return half_copy(place, index, c, sib_send.at[place, index], sibling)

    def host_copy(place, index):
        return half_copy(place, index, c, fwd_send.at[place, index], other_host)

    def leads_at(place):
        return (leads_even if place % 2 == 0 else 1 - leads_even) == 1

    def forward(place):
        for index in range(3):
            sibling_copy(place, index).wait_recv()

            @pl.when(leads_at(place))
            def _():
                host_copy(place, index).start()

            sibling_copy(place, index).start()

    def wait_sibling(place):
        for index in range(3):
            half_copy(place, index, 1 - c, sib_send.at[place, index], sibling).wait_recv()

    n_src = EXPERTS

    def split(stacked):
        blocks = stacked.reshape(n_src, BLOCK, hidden)
        return (
            blocks[:, :CAP].reshape(n_src * CAP, hidden),
            blocks[:, CAP:].reshape(n_src * CAP, hidden),
        )

    def send_back(acc, out, send, recv, section, into):
        for dist in (3, 2, 1, 0):
            for src_yh in range(2):
                q = dist * 2 + src_yh
                both = jnp.concatenate(
                    [acc[q * CAP:(q + 1) * CAP, :half], acc[q * CAP:(q + 1) * CAP, half:]], axis=0
                )
                out[q * BLOCK:(q + 1) * BLOCK, :] = both.astype(BF16)
                back_copy(q, out, send, recv, section, into).start()

    def back_copy(q, out, send, recv, section, into):
        return remote(
            row_block(out, q), row_block(into, host_expert), send.at[q], recv.at[host_expert],
            section, source(q // 2, q % 2),
        )

    up_args = (back_up_out, up_send, up_recv, after, back_up_in)
    dn_args = (back_dn_out, dn_send, dn_recv, before, back_dn_in)

    def use_slice(place, last):
        x = rows_in[:, :features]
        gate_up, gate_dn = split(jnp.dot(x, wg[place], preferred_element_type=F32))
        upper_up, upper_dn = split(jnp.dot(x, wu[place], preferred_element_type=F32))
        middle = (jax.nn.silu(gate_up) * upper_up).astype(BF16)

        def add_up(step, _):
            at = pl.ds(pl.multiple_of(step * width, width), width)
            acc_up[:, at] += jnp.dot(middle, wd[place, :, at], preferred_element_type=F32)
            return 0

        lax.fori_loop(0, features // width, add_up, 0)
        if last:
            send_back(acc_up, *up_args)

        g_rows = rows_in[:, features:]
        low, _ = split(contract_last(g_rows, wd[place, :, :half]))
        _, high = split(contract_last(g_rows, wd[place, :, half:]))
        pulled = low + high
        sigma = jax.nn.sigmoid(gate_dn)
        d_gate = (pulled * upper_dn * sigma * (1.0 + gate_dn * (1.0 - sigma))).astype(BF16)
        d_upper = (pulled * gate_dn * sigma).astype(BF16)

        def add_dn(step, _):
            at = pl.ds(pl.multiple_of(step * width, width), width)
            acc_dn[:, at] += contract_last(d_gate, wg[place, at, :]) + contract_last(d_upper, wu[place, at, :])
            return 0

        lax.fori_loop(0, features // width, add_dn, 0)
        if last:
            send_back(acc_dn, *dn_args)

    forward(0)
    forward(1)
    forward(2)
    for slot in range(n_src):
        remote(
            row_block(rows_in, slot), row_block(rows_in, slot), row_send.at[slot], row_recv.at[slot], sec, sibling
        ).wait_recv()
    for place in range(3):
        wait_sibling(place)

    def early(place, _):
        use_slice(place, False)
        return 0

    lax.fori_loop(0, 3, early, 0)
    forward(3)
    wait_sibling(3)
    use_slice(3, True)

    for copy in residuals:
        copy.wait_recv()

    def unpick(route_row):
        lane = lax.broadcasted_iota(jnp.int32, (tokens, n_rows), 1).astype(F32)
        at = column(block_rows(route_row))
        return jnp.concatenate([lane == at, lane == at + float(CAP)], axis=0).astype(BF16)

    def wait_back(out, send, recv, section, into):
        for g in range(EXPERTS):
            remote(
                row_block(into, g), row_block(into, g), send.at[g], recv.at[g], section, me
            ).wait_recv()

    wait_back(*up_args)
    pick_up = unpick(meta_up_in[0:1, :])
    gate_up_col = column(meta_up_in[1:2, :])

    def finish_up(step, _):
        at = pl.ds(pl.multiple_of(step * width, width), width)
        back = jnp.dot(pick_up, back_up_in[:, at], preferred_element_type=F32)
        for h in range(2):
            to = pl.ds(pl.multiple_of(h * half + step * width, width), width)
            mixed = back[h * tokens:(h + 1) * tokens] * gate_up_col
            out_up[:, to] = (act_in[:, to].astype(F32) + mixed).astype(BF16)
        return 0

    lax.fori_loop(0, half // width, finish_up, 0)

    wait_back(*dn_args)
    pick_dn = unpick(meta_dn_in[2:3, :])
    gate_dn_col = column(meta_dn_in[3:4, :])

    def pull_dn(step, carry):
        squares, dots = carry
        at = pl.ds(pl.multiple_of(step * width, width), width)
        back = jnp.dot(pick_dn, back_dn_in[:, at], preferred_element_type=F32)
        for h in range(2):
            to = pl.ds(pl.multiple_of(h * half + step * width, width), width)
            u = back[h * tokens:(h + 1) * tokens] * gate_dn_col * gain_in[0:1, to]
            acc_dn[:tokens, to] = u
            x = saved_in[:, to].astype(F32)
            squares = squares + jnp.sum(x * x, axis=-1, keepdims=True)
            dots = dots + jnp.sum(x * u, axis=-1, keepdims=True)
        return squares, dots

    zero = jnp.zeros((tokens, 1), F32)
    squares, dots = lax.fori_loop(0, half // width, pull_dn, (zero, zero))
    r = lax.rsqrt(squares / features + EPS)
    pull = r * r * r * (dots / features)

    def finish_dn(step, _):
        to = pl.ds(pl.multiple_of(step * width, width), width)
        x = saved_in[:, to].astype(F32)
        out_dn[:, to] = (grad_in[:, to].astype(F32) + r * acc_dn[:tokens, to] - x * pull).astype(BF16)
        return 0

    lax.fori_loop(0, features // width, finish_dn, 0)

    for index in range(3):
        for h in range(2):

            @pl.when(jnp.logical_not(jnp.logical_and(own_host == z, c == h)))
            def _():
                slice_copy(index, h).wait_send()

    for g in range(EXPERTS):
        peer, copy = row_copy(g)

        @pl.when(peer != me)
        def _():
            copy.wait_send()

    for copy in residuals:
        copy.wait_send()
    for place in range(4):
        for index in range(3):
            sibling_copy(place, index).wait_send()

            @pl.when(leads_at(place))
            def _():
                host_copy(place, index).wait_send()

    for q in range(n_src):
        back_copy(q, *up_args).wait_send()
        back_copy(q, *dn_args).wait_send()


def per_device(
    act_up, routes_up, gates_up, saved_down, grad_down, routes_down, gates_down, norm_gain, w_gate, w_up, w_down,
):
    tokens, features = act_up.shape[1:]
    hidden = w_gate.shape[3]
    half = features // 2
    rows = EXPERTS * BLOCK
    meta = jnp.concatenate(
        [
            routes_up.reshape(1, tokens).astype(F32),
            gates_up.reshape(1, tokens),
            routes_down.reshape(1, tokens).astype(F32),
            gates_down.reshape(1, tokens),
            jnp.zeros((4, tokens), F32),
        ],
        axis=0,
    )
    vmem = pl.BlockSpec(memory_space=pltpu.VMEM)
    hbm = pl.BlockSpec(memory_space=pl.ANY)
    dma = pltpu.SemaphoreType.DMA
    up, down = pl.pallas_call(
        kernel,
        out_shape=(jax.ShapeDtypeStruct((tokens, features), BF16),) * 2,
        in_specs=[vmem] * 5 + [hbm] * 3,
        out_specs=(vmem, vmem),
        scratch_shapes=[
            pltpu.VMEM((SLICES, features, hidden), BF16),
            pltpu.VMEM((SLICES, features, hidden), BF16),
            pltpu.VMEM((SLICES, hidden, features), BF16),
            pltpu.VMEM((2 * tokens, features + half), BF16),
            pltpu.VMEM((rows, features + half), BF16),
            pltpu.VMEM((rows, features + half), BF16),
            pltpu.VMEM((EXPERTS * CAP, features), F32),
            pltpu.VMEM((EXPERTS * CAP, features), F32),
            pltpu.VMEM((rows, half), BF16),
            pltpu.VMEM((rows, half), BF16),
            pltpu.VMEM((rows, half), BF16),
            pltpu.VMEM((rows, half), BF16),
            pltpu.VMEM((tokens, features), BF16),
            pltpu.VMEM((tokens, features), BF16),
            pltpu.VMEM((tokens, features), BF16),
            pltpu.VMEM((1, features), F32),
            pltpu.VMEM((8, tokens), F32),
            pltpu.VMEM((8, tokens), F32),
            dma((EXPERTS,)),
            dma((EXPERTS,)),
            dma((3, 2)),
            dma((SLICES, 3, 2)),
            dma((SLICES, 3)),
            dma((SLICES, 3)),
            dma((EXPERTS,)),
            dma((EXPERTS,)),
            dma((EXPERTS,)),
            dma((EXPERTS,)),
            dma((6,)),
            dma((6,)),
        ],
        compiler_params=pltpu.CompilerParams(
            collective_id=0, has_side_effects=True, vmem_limit_bytes=60 * MIB
        ),
        cost_estimate=pl.CostEstimate(flops=12_000_000_000, bytes_accessed=12_000_000, transcendentals=400_000),
    )(
        act_up[0], saved_down[0], grad_down[0], norm_gain, meta, w_gate[0, 0], w_up[0, 0], w_down[0, 0],
    )
    return up[None], down[None]


def solution(mesh):
    tokens = P("section", "expert", None)
    weights = P("section", "expert", None, None)
    return jax.shard_map(
        per_device,
        mesh=mesh,
        in_specs=(tokens,) * 7 + (P("section", None),) + (weights,) * 3,
        out_specs=(tokens, tokens),
        check_vma=False,
    )
```

time: 755 us -> 454 us (0.60)
  Pallas kernels: 0 us -> 442 us
  blocking collectives: 372 us -> 0 us
  waiting for transfers between devices: 276 us -> 0 us
  matrix products: 39.9 us -> 0 us
  other arithmetic: 34.9 us -> 0.68 us
  local copies, waits for them, and re-layouts: 19.5 us -> 4.44 us
  starting transfers between devices: 7.98 us -> 0 us
    pallas_call x0 -> x1, Pallas kernels: none -> 442 us  [per_device(): pl.pallas_call(kernel, out_shape=(jax.ShapeDtypeStruct((tokens, features)...]
    all_to_all x1 -> x0, blocking collectives: 372 us -> none  [per_device(): lax.all_to_all(jnp.tile(outgoing, (SLICES, 1, 1)), 'expert', split_axis=0...]
    all_to_all x1 -> x0, waiting for transfers between devices: 240 us -> none  [per_device(): lax.all_to_all(computed.reshape(groups, item_count, 2 * features), 'exper...]
    dot_general x8 -> x0, matrix products: 39.9 us -> none  [the longest x3 22.9 us: contract_last(): lax.dot_general(matrix, weights, (((1,), (1,)), ((), ())), preferred_elem...]
    ppermute x2 -> x0, waiting for transfers between devices: 35.9 us -> none  [shifted(): lax.ppermute(array, axis, [(i, (i + by) % size) for i in range(size)])]
    reduce_sum x6 -> x0, other arithmetic: 16.2 us -> none  [the longest x1 9.06 us: per_device(): jnp.sum(returned_rows.astype(jnp.float32).reshape(SLICES, slot_total, 2 *...]
    concatenate x2 -> x0, other arithmetic: 9.86 us -> none  [the longest x1 9.59 us: expert_rows(): return jnp.concatenate([forward_part, backward_part], axis=1)]
  transfers between devices with their start and end apart: 3 -> 0, of which waited for: 3 -> 0; matrix products, arithmetic and copies ran while one was open for 1% -> 0% of each run, Pallas kernels for 0% -> 0%
where the time goes in v1:
time: 454 us; the launch traced here: 448 us
  Pallas kernels  442 us (97%)
    pallas_call x1, Pallas kernels, per_device(): pl.pallas_call(kernel, out_shape=(jax.ShapeDtypeStruct((tokens, features)...  442 us

profile of v1, /device:TPU:25, one launch (start us, length us, event | category | flops | bytes accessed | tf_op | source)
XLA Modules:
  0.0 447.5 jit_solution(1519394438655731596)
XLA Ops:
  0.6 0.7 convert_bitcast_fusion
  1.3 1.3 concatenate.3.meta
  2.6 441.7 %shard_map.122 = (bf16[128,3584]{1,0:T(8,128)(2,1)}, bf16[128,3584]{1,0:T(8,128)(2,1)}) custom-call(bf16[128,3584]{1,0:T(8,128)(2,1)} %bitcast.21, bf16[128,3584]{1,0:T(8,128)(2,1)} %bitcast.22, bf16[128,3584]{1,0:T(8,128)(2,1)} %bitcast.23, f32[1,3584]{1,0:T(1,128)} %gain.1, f32[8,128]{1,0:T(8,128)} %concatenate.3.meta, bf16[3584,256]{1,0:T(8,128)(2,1)} %bitcast.18, ...), custom_call_target="tpu_custom_call" | custom-call | flops 12000000000 | bytes 12000000 | tf_op jit(solution)/shard_map/pallas_call | solution.py:448
  444.3 0.0 copy-start
  444.3 2.2 copy.15
  446.6 0.0 copy-done
  446.6 0.9 copy.16
  (1 shorter events, 0.0 us)
Async XLA Ops:
  444.3 2.3 copy-start

commit v2 on v1

--- a/solution.py
+++ b/solution.py
@@ -225,8 +225,6 @@
         remote(gain, gain_in, res_send.at[4], res_recv.at[4], before, me),
         remote(meta, meta_dn_in, res_send.at[5], res_recv.at[5], before, me),
     ]
-    for copy in residuals:
-        copy.start()
 
     acc_up[...] = jnp.zeros_like(acc_up)
     acc_dn[...] = jnp.zeros_like(acc_dn)
@@ -238,21 +236,25 @@
     def sibling_copy(place, index):
         return half_copy(place, index, c, sib_send.at[place, index], sibling)
 
-    def host_copy(place, index):
-        return half_copy(place, index, c, fwd_send.at[place, index], other_host)
-
-    def leads_at(place):
-        return (leads_even if place % 2 == 0 else 1 - leads_even) == 1
-
-    def forward(place):
+    def host_copy(n, index):
+        return half_copy(lead_place(n), index, c, fwd_send.at[n, index], other_host)
+
+    def lead_place(n):
+        return 2 * n + 1 - leads_even
+
+    def follow_place(n):
+        return 2 * n + leads_even
+
+    def lead(n):
         for index in range(3):
-            sibling_copy(place, index).wait_recv()
-
-            @pl.when(leads_at(place))
-            def _():
-                host_copy(place, index).start()
-
-            sibling_copy(place, index).start()
+            sibling_copy(lead_place(n), index).wait_recv()
+            host_copy(n, index).start()
+            sibling_copy(lead_place(n), index).start()
+
+    def follow(n):
+        for index in range(3):
+            sibling_copy(follow_place(n), index).wait_recv()
+            sibling_copy(follow_place(n), index).start()
 
     def wait_sibling(place):
         for index in range(3):
@@ -318,24 +320,27 @@
         if last:
             send_back(acc_dn, *dn_args)
 
-    forward(0)
-    forward(1)
-    forward(2)
+    lead(0)
+    lead(1)
+    follow(0)
+    for copy in residuals:
+        copy.start()
+
     for slot in range(n_src):
         remote(
             row_block(rows_in, slot), row_block(rows_in, slot), row_send.at[slot], row_recv.at[slot], sec, sibling
         ).wait_recv()
-    for place in range(3):
+    for place in (lead_place(0), lead_place(1), follow_place(0)):
         wait_sibling(place)
 
-    def early(place, _):
-        use_slice(place, False)
+    def early(step, _):
+        use_slice((step // 2) * lead_place(1) + (1 - step // 2) * (lead_place(0) + lax.rem(step, 2) * (2 * leads_even - 1)), False)
         return 0
 
     lax.fori_loop(0, 3, early, 0)
-    forward(3)
-    wait_sibling(3)
-    use_slice(3, True)
+    follow(1)
+    wait_sibling(follow_place(1))
+    use_slice(follow_place(1), True)
 
     for copy in residuals:
         copy.wait_recv()
@@ -415,11 +420,9 @@
     for place in range(4):
         for index in range(3):
             sibling_copy(place, index).wait_send()
-
-            @pl.when(leads_at(place))
-            def _():
-                host_copy(place, index).wait_send()
-
+    for n in range(2):
+        for index in range(3):
+            host_copy(n, index).wait_send()
     for q in range(n_src):
         back_copy(q, *up_args).wait_send()
         back_copy(q, *dn_args).wait_send()
@@ -474,7 +477,7 @@
             dma((3, 2)),
             dma((SLICES, 3, 2)),
             dma((SLICES, 3)),
-            dma((SLICES, 3)),
+            dma((2, 3)),
             dma((EXPERTS,)),
             dma((EXPERTS,)),
             dma((EXPERTS,)),

time: 454 us -> 328 us (0.72)
  Pallas kernels: 442 us -> 319 us
    pallas_call x1, Pallas kernels: 442 us -> 319 us  [per_device(): pl.pallas_call(kernel, out_shape=(jax.ShapeDtypeStruct((tokens, features)...]
where the time goes in v2:
time: 328 us; the launch traced here: 325 us
  Pallas kernels  319 us (97%)
  local copies, waits for them, and re-layouts  4.44 us (1%)
    pallas_call x1, Pallas kernels, per_device(): pl.pallas_call(kernel, out_shape=(jax.ShapeDtypeStruct((tokens, features)...  319 us

profile of v2, /device:TPU:25, one launch (start us, length us, event | category | flops | bytes accessed | tf_op | source)
XLA Modules:
  0.0 324.7 jit_solution(2938693173381441863)
XLA Ops:
  0.6 0.7 convert_bitcast_fusion
  1.3 1.3 concatenate.3.meta
  2.6 318.9 %shard_map.122 = (bf16[128,3584]{1,0:T(8,128)(2,1)}, bf16[128,3584]{1,0:T(8,128)(2,1)}) custom-call(bf16[128,3584]{1,0:T(8,128)(2,1)} %bitcast.21, bf16[128,3584]{1,0:T(8,128)(2,1)} %bitcast.22, bf16[128,3584]{1,0:T(8,128)(2,1)} %bitcast.23, f32[1,3584]{1,0:T(1,128)} %gain.1, f32[8,128]{1,0:T(8,128)} %concatenate.3.meta, bf16[3584,256]{1,0:T(8,128)(2,1)} %bitcast.18, ...), custom_call_target="tpu_custom_call" | custom-call | flops 12000000000 | bytes 12000000 | tf_op jit(solution)/shard_map/pallas_call | solution.py:451
  321.5 0.0 copy-start
  321.5 2.2 copy.15
  323.8 0.0 copy-done
  323.8 0.9 copy.16
  (1 shorter events, 0.0 us)
Async XLA Ops:
  321.5 2.3 copy-start

commit v3 on v2

--- a/solution.py
+++ b/solution.py
@@ -50,7 +50,7 @@
 def kernel(
     act, saved, grad, gain, meta, wg_in, wu_in, wd_in,
     out_up, out_dn,
-    wg, wu, wd, table, packed, rows_in, acc_up, acc_dn,
+    wg, wu, wd, table_up, table_dn, packed_up, packed_dn, rows_up, rows_dn, x_up, x_dn, g_dn, acc_up, acc_dn,
     back_up_out, back_dn_out, back_up_in, back_dn_in,
     act_in, saved_in, grad_in, gain_in, meta_up_in, meta_dn_in,
     row_send, row_recv, src_send, w_recv, sib_send, fwd_send,
@@ -165,57 +165,78 @@
     gain_row = gain[...]
     rows_step = 16
 
-    def norm_rows(step, _):
+    def normed(ref, at):
+        values = ref[at, :].astype(F32)
+        scaling = lax.rsqrt(jnp.mean(values * values, axis=-1, keepdims=True) + EPS)
+        return (values * scaling * gain_row).astype(BF16)
+
+    def norm_up(step, _):
         at = pl.ds(pl.multiple_of(step * rows_step, rows_step), rows_step)
-        for source_ref, base in ((act, 0), (saved, tokens)):
-            values = source_ref[at, :].astype(F32)
-            scaling = lax.rsqrt(jnp.mean(values * values, axis=-1, keepdims=True) + EPS)
-            to = pl.ds(pl.multiple_of(base + step * rows_step, rows_step), rows_step)
-            table[to, :features] = (values * scaling * gain_row).astype(BF16)
+        to = pl.ds(pl.multiple_of(tokens + step * rows_step, rows_step), rows_step)
+        rows = normed(act, at)
+        table_up[at, :] = rows[:, :half]
+        table_up[to, :] = rows[:, half:]
         return 0
 
-    lax.fori_loop(0, tokens // rows_step, norm_rows, 0)
-    table[:tokens, features:] = grad[:, :half]
-    table[tokens:, features:] = grad[:, half:]
-
-    at_up = block_rows(meta[0:1, :])
-    at_dn = block_rows(meta[2:3, :])
+    def norm_dn(step, _):
+        at = pl.ds(pl.multiple_of(step * rows_step, rows_step), rows_step)
+        table_dn[at, :] = normed(saved, at)
+        return 0
+
     n_rows = EXPERTS * BLOCK
-    row_index = lax.broadcasted_iota(jnp.int32, (n_rows, 2 * tokens), 0).astype(F32)
-    pick_h = (row_index == jnp.concatenate([at_up, at_dn + float(CAP)], axis=1)).astype(BF16)
-    pick_g = (row_index == jnp.concatenate([at_dn, at_dn + float(CAP)], axis=1)).astype(BF16)
     width = 256
 
-    def pack(first, pick):
+    def pack(route_row, table, packed):
+        at = block_rows(route_row)
+        row_index = lax.broadcasted_iota(jnp.int32, (n_rows, 2 * tokens), 0).astype(F32)
+        pick = (row_index == jnp.concatenate([at, at + float(CAP)], axis=1)).astype(BF16)
+
         def body(step, _):
-            at = pl.ds(pl.multiple_of(first + step * width, width), width)
+            at = pl.ds(pl.multiple_of(step * width, width), width)
             packed[:, at] = jnp.dot(pick, table[:, at], preferred_element_type=F32).astype(BF16)
             return 0
 
-        return body
-
-    lax.fori_loop(0, features // width, pack(0, pick_h), 0)
-    lax.fori_loop(0, half // width, pack(features, pick_g), 0)
+        lax.fori_loop(0, packed.shape[1] // width, body, 0)
 
     def row_block(ref, index):
         return ref.at[pl.ds(pl.multiple_of(index * BLOCK, BLOCK), BLOCK)]
 
-    def row_copy(g):
+    kinds = ((packed_up, rows_up), (packed_dn, rows_dn))
+
+    def row_copy(kind, g):
+        packed, rows = kinds[kind]
         peer, slot = host_of(g)
         return peer, remote(
-            row_block(packed, g), row_block(rows_in, slot), row_send.at[g], row_recv.at[slot], sec, peer
+            row_block(packed, g), row_block(rows, slot), row_send.at[kind, g], row_recv.at[kind, slot], sec, peer
         )
 
-    for g in range(EXPERTS):
-        peer, slot = host_of(g)
-
-        @pl.when(peer == me)
-        def _():
-            pltpu.make_async_copy(row_block(packed, g), row_block(rows_in, slot), row_recv.at[slot]).start()
-
-        @pl.when(peer != me)
-        def _():
-            row_copy(g)[1].start()
+    def send_rows(kind):
+        packed, rows = kinds[kind]
+        for g in range(EXPERTS):
+            peer, slot = host_of(g)
+
+            @pl.when(peer == me)
+            def _():
+                pltpu.make_async_copy(
+                    row_block(packed, g), row_block(rows, slot), row_recv.at[kind, slot]
+                ).start()
+
+            @pl.when(peer != me)
+            def _():
+                row_copy(kind, g)[1].start()
+
+    def wait_rows(kind):
+        rows = kinds[kind][1]
+        for slot in range(EXPERTS):
+            view = row_block(rows, slot)
+            remote(view, view, row_send.at[kind, slot], row_recv.at[kind, slot], sec, sibling).wait_recv()
+
+    lax.fori_loop(0, tokens // rows_step, norm_up, 0)
+    pack(meta[0:1, :], table_up, packed_up)
+    send_rows(0)
+    lax.fori_loop(0, tokens // rows_step, norm_dn, 0)
+    table_dn[tokens:, :] = grad[...]
+    pack(meta[2:3, :], table_dn, packed_dn)
 
     residuals = [
         remote(act, act_in, res_send.at[0], res_recv.at[0], after, me),
@@ -262,12 +283,20 @@
 
     n_src = EXPERTS
 
-    def split(stacked):
-        blocks = stacked.reshape(n_src, BLOCK, hidden)
-        return (
-            blocks[:, :CAP].reshape(n_src * CAP, hidden),
-            blocks[:, CAP:].reshape(n_src * CAP, hidden),
-        )
+    def arrange(rows, low, high):
+        def body(step, _):
+            top = rows[pl.ds(pl.multiple_of(step * 2 * BLOCK, 2 * BLOCK), BLOCK), :].astype(F32)
+            bottom = rows[pl.ds(pl.multiple_of((step * 2 + 1) * BLOCK, BLOCK), BLOCK), :].astype(F32)
+            at = pl.ds(pl.multiple_of(step * BLOCK, BLOCK), BLOCK)
+            low[at, :rows.shape[1]] = jnp.concatenate([top[:CAP], bottom[:CAP]], axis=0).astype(BF16)
+            second = jnp.concatenate([top[CAP:], bottom[CAP:]], axis=0).astype(BF16)
+            if high is None:
+                low[at, rows.shape[1]:] = second
+            else:
+                high[at, :] = second
+            return 0
+
+        lax.fori_loop(0, n_src // 2, body, 0)
 
     def send_back(acc, out, send, recv, section, into):
         for dist in (3, 2, 1, 0):
@@ -288,11 +317,11 @@
     up_args = (back_up_out, up_send, up_recv, after, back_up_in)
     dn_args = (back_dn_out, dn_send, dn_recv, before, back_dn_in)
 
-    def use_slice(place, last):
-        x = rows_in[:, :features]
-        gate_up, gate_dn = split(jnp.dot(x, wg[place], preferred_element_type=F32))
-        upper_up, upper_dn = split(jnp.dot(x, wu[place], preferred_element_type=F32))
-        middle = (jax.nn.silu(gate_up) * upper_up).astype(BF16)
+    def use_up(place):
+        x = x_up[...]
+        gate = jnp.dot(x, wg[place], preferred_element_type=F32)
+        upper = jnp.dot(x, wu[place], preferred_element_type=F32)
+        middle = (jax.nn.silu(gate) * upper).astype(BF16)
 
         def add_up(step, _):
             at = pl.ds(pl.multiple_of(step * width, width), width)
@@ -300,16 +329,15 @@
             return 0
 
         lax.fori_loop(0, features // width, add_up, 0)
-        if last:
-            send_back(acc_up, *up_args)
-
-        g_rows = rows_in[:, features:]
-        low, _ = split(contract_last(g_rows, wd[place, :, :half]))
-        _, high = split(contract_last(g_rows, wd[place, :, half:]))
-        pulled = low + high
-        sigma = jax.nn.sigmoid(gate_dn)
-        d_gate = (pulled * upper_dn * sigma * (1.0 + gate_dn * (1.0 - sigma))).astype(BF16)
-        d_upper = (pulled * gate_dn * sigma).astype(BF16)
+
+    def use_dn(place):
+        x = x_dn[...]
+        gate = jnp.dot(x, wg[place], preferred_element_type=F32)
+        upper = jnp.dot(x, wu[place], preferred_element_type=F32)
+        pulled = contract_last(g_dn[...], wd[place])
+        sigma = jax.nn.sigmoid(gate)
+        d_gate = (pulled * upper * sigma * (1.0 + gate * (1.0 - sigma))).astype(BF16)
+        d_upper = (pulled * gate * sigma).astype(BF16)
 
         def add_dn(step, _):
             at = pl.ds(pl.multiple_of(step * width, width), width)
@@ -317,30 +345,37 @@
             return 0
 
         lax.fori_loop(0, features // width, add_dn, 0)
-        if last:
-            send_back(acc_dn, *dn_args)
+
+    def at_step(step):
+        return 2 * (step // 2) + 1 - leads_even + lax.rem(step, 2) * (2 * leads_even - 1)
+
+    def loop(use, first, end):
+        def body(step, _):
+            use(at_step(step))
+            return 0
+
+        lax.fori_loop(first, end, body, 0)
 
     lead(0)
     lead(1)
+    send_rows(1)
     follow(0)
     for copy in residuals:
         copy.start()
 
-    for slot in range(n_src):
-        remote(
-            row_block(rows_in, slot), row_block(rows_in, slot), row_send.at[slot], row_recv.at[slot], sec, sibling
-        ).wait_recv()
+    wait_rows(0)
+    arrange(rows_up, x_up, None)
     for place in (lead_place(0), lead_place(1), follow_place(0)):
         wait_sibling(place)
-
-    def early(step, _):
-        use_slice((step // 2) * lead_place(1) + (1 - step // 2) * (lead_place(0) + lax.rem(step, 2) * (2 * leads_even - 1)), False)
-        return 0
-
-    lax.fori_loop(0, 3, early, 0)
+    loop(use_up, 0, 3)
     follow(1)
     wait_sibling(follow_place(1))
-    use_slice(follow_place(1), True)
+    loop(use_up, 3, 4)
+    send_back(acc_up, *up_args)
+    wait_rows(1)
+    arrange(rows_dn, x_dn, g_dn)
+    loop(use_dn, 0, 4)
+    send_back(acc_dn, *dn_args)
 
     for copy in residuals:
         copy.wait_recv()
@@ -408,12 +443,12 @@
             def _():
                 slice_copy(index, h).wait_send()
 
-    for g in range(EXPERTS):
-        peer, copy = row_copy(g)
-
-        @pl.when(peer != me)
-        def _():
-            copy.wait_send()
+    for kind in range(2):
+        for g in range(EXPERTS):
+
+            @pl.when(host_of(g)[0] != me)
+            def _():
+                row_copy(kind, g)[1].wait_send()
 
     for copy in residuals:
         copy.wait_send()
@@ -457,9 +492,15 @@
             pltpu.VMEM((SLICES, features, hidden), BF16),
             pltpu.VMEM((SLICES, features, hidden), BF16),
             pltpu.VMEM((SLICES, hidden, features), BF16),
-            pltpu.VMEM((2 * tokens, features + half), BF16),
-            pltpu.VMEM((rows, features + half), BF16),
-            pltpu.VMEM((rows, features + half), BF16),
+            pltpu.VMEM((2 * tokens, half), BF16),
+            pltpu.VMEM((2 * tokens, features), BF16),
+            pltpu.VMEM((rows, half), BF16),
+            pltpu.VMEM((rows, features), BF16),
+            pltpu.VMEM((rows, half), BF16),
+            pltpu.VMEM((rows, features), BF16),
+            pltpu.VMEM((EXPERTS * CAP, features), BF16),
+            pltpu.VMEM((EXPERTS * CAP, features), BF16),
+            pltpu.VMEM((EXPERTS * CAP, features), BF16),
             pltpu.VMEM((EXPERTS * CAP, features), F32),
             pltpu.VMEM((EXPERTS * CAP, features), F32),
             pltpu.VMEM((rows, half), BF16),
@@ -472,8 +513,8 @@
             pltpu.VMEM((1, features), F32),
             pltpu.VMEM((8, tokens), F32),
             pltpu.VMEM((8, tokens), F32),
-            dma((EXPERTS,)),
-            dma((EXPERTS,)),
+            dma((2, EXPERTS)),
+            dma((2, EXPERTS)),
             dma((3, 2)),
             dma((SLICES, 3, 2)),
             dma((SLICES, 3)),

time: 328 us -> 314 us (0.957)
  Pallas kernels: 319 us -> 304 us
    pallas_call x1, Pallas kernels: 319 us -> 304 us  [per_device(): pl.pallas_call(kernel, out_shape=(jax.ShapeDtypeStruct((tokens, features)...]
where the time goes in v3:
time: 314 us; the launch traced here: 310 us
  Pallas kernels  304 us (97%)
  local copies, waits for them, and re-layouts  4.44 us (1%)
    pallas_call x1, Pallas kernels, per_device(): pl.pallas_call(kernel, out_shape=(jax.ShapeDtypeStruct((tokens, features)...  304 us

profile of v3, /device:TPU:25, one launch (start us, length us, event | category | flops | bytes accessed | tf_op | source)
XLA Modules:
  0.0 310.2 jit_solution(9519308504329812498)
XLA Ops:
  0.6 0.7 convert_bitcast_fusion
  1.3 1.3 concatenate.3.meta
  2.6 304.4 %shard_map.122 = (bf16[128,3584]{1,0:T(8,128)(2,1)}, bf16[128,3584]{1,0:T(8,128)(2,1)}) custom-call(bf16[128,3584]{1,0:T(8,128)(2,1)} %bitcast.21, bf16[128,3584]{1,0:T(8,128)(2,1)} %bitcast.22, bf16[128,3584]{1,0:T(8,128)(2,1)} %bitcast.23, f32[1,3584]{1,0:T(1,128)} %gain.1, f32[8,128]{1,0:T(8,128)} %concatenate.3.meta, bf16[3584,256]{1,0:T(8,128)(2,1)} %bitcast.18, ...), custom_call_target="tpu_custom_call" | custom-call | flops 12000000000 | bytes 12000000 | tf_op jit(solution)/shard_map/pallas_call | solution.py:486
  307.0 0.0 copy-start
  307.0 2.2 copy.15
  309.2 0.0 copy-done
  309.2 0.9 copy.16
  (1 shorter events, 0.0 us)
Async XLA Ops:
  307.0 2.3 copy-start

commit v4 on v3

--- a/solution.py
+++ b/solution.py
@@ -48,11 +48,11 @@
 
 
 def kernel(
-    act, saved, grad, gain, meta, wg_in, wu_in, wd_in,
+    act, saved, grad, gain, route_up, weight_up, route_dn, weight_dn, wg_in, wu_in, wd_in,
     out_up, out_dn,
     wg, wu, wd, table_up, table_dn, packed_up, packed_dn, rows_up, rows_dn, x_up, x_dn, g_dn, acc_up, acc_dn,
     back_up_out, back_dn_out, back_up_in, back_dn_in,
-    act_in, saved_in, grad_in, gain_in, meta_up_in, meta_dn_in,
+    act_in, saved_in, grad_in, gain_in, route_up_in, weight_up_in, route_dn_in, weight_dn_in,
     row_send, row_recv, src_send, w_recv, sib_send, fwd_send,
     up_send, up_recv, dn_send, dn_recv, res_send, res_recv,
 ):
@@ -119,15 +119,8 @@
 
     greet(sec, other_host)
     greet(sec, sibling)
-    for g in range(EXPERTS):
-        peer, _ = host_of(g)
-        greet(before, peer)
-        greet(after, peer)
     greet(before, me)
     greet(after, me)
-    here = jnp.where(own_host == z, 1, 0)
-    pl.semaphore_wait(barrier, 29 - here)
-
     mats = ((wg_in, wg), (wu_in, wu), (wd_in, wd))
 
     def w_half(ref, index, h):
@@ -139,28 +132,6 @@
             src_ref=src, dst_ref=dst, send_sem=send, recv_sem=recv,
             device_id=(section, peer), device_id_type=MESH,
         )
-
-    def slice_copy(index, h):
-        src, dst = mats[index]
-        return remote(
-            w_half(src, index, h), w_half(dst.at[own_place], index, h),
-            src_send.at[index, h], w_recv.at[own_place, index, h], sec, own_host * 4 + yh * 2 + h,
-        )
-
-    for index in range(3):
-        for h in range(2):
-            mine = jnp.logical_and(own_host == z, c == h)
-
-            @pl.when(mine)
-            def _():
-                src, dst = mats[index]
-                pltpu.make_async_copy(
-                    w_half(src, index, h), w_half(dst.at[own_place], index, h), w_recv.at[own_place, index, h]
-                ).start()
-
-            @pl.when(jnp.logical_not(mine))
-            def _():
-                slice_copy(index, h).start()
 
     gain_row = gain[...]
     rows_step = 16
@@ -232,19 +203,46 @@
             remote(view, view, row_send.at[kind, slot], row_recv.at[kind, slot], sec, sibling).wait_recv()
 
     lax.fori_loop(0, tokens // rows_step, norm_up, 0)
-    pack(meta[0:1, :], table_up, packed_up)
+    pack(route_up[...].astype(F32), table_up, packed_up)
+    here = jnp.where(own_host == z, 1, 0)
+    pl.semaphore_wait(barrier, 13 - here)
+
+    def slice_copy(index, h):
+        src, dst = mats[index]
+        return remote(
+            w_half(src, index, h), w_half(dst.at[own_place], index, h),
+            src_send.at[index, h], w_recv.at[own_place, index, h], sec, own_host * 4 + yh * 2 + h,
+        )
+
+    for index in range(3):
+        for h in range(2):
+            mine = jnp.logical_and(own_host == z, c == h)
+
+            @pl.when(mine)
+            def _():
+                src, dst = mats[index]
+                pltpu.make_async_copy(
+                    w_half(src, index, h), w_half(dst.at[own_place], index, h), w_recv.at[own_place, index, h]
+                ).start()
+
+            @pl.when(jnp.logical_not(mine))
+            def _():
+                slice_copy(index, h).start()
+
     send_rows(0)
     lax.fori_loop(0, tokens // rows_step, norm_dn, 0)
     table_dn[tokens:, :] = grad[...]
-    pack(meta[2:3, :], table_dn, packed_dn)
+    pack(route_dn[...].astype(F32), table_dn, packed_dn)
 
     residuals = [
         remote(act, act_in, res_send.at[0], res_recv.at[0], after, me),
-        remote(meta, meta_up_in, res_send.at[1], res_recv.at[1], after, me),
+        remote(route_up, route_up_in, res_send.at[1], res_recv.at[1], after, me),
+        remote(weight_up, weight_up_in, res_send.at[6], res_recv.at[6], after, me),
         remote(saved, saved_in, res_send.at[2], res_recv.at[2], before, me),
         remote(grad, grad_in, res_send.at[3], res_recv.at[3], before, me),
         remote(gain, gain_in, res_send.at[4], res_recv.at[4], before, me),
-        remote(meta, meta_dn_in, res_send.at[5], res_recv.at[5], before, me),
+        remote(route_dn, route_dn_in, res_send.at[5], res_recv.at[5], before, me),
+        remote(weight_dn, weight_dn_in, res_send.at[7], res_recv.at[7], before, me),
     ]
 
     acc_up[...] = jnp.zeros_like(acc_up)
@@ -298,8 +296,8 @@
 
         lax.fori_loop(0, n_src // 2, body, 0)
 
-    def send_back(acc, out, send, recv, section, into):
-        for dist in (3, 2, 1, 0):
+    def send_back(dists, acc, out, send, recv, section, into):
+        for dist in dists:
             for src_yh in range(2):
                 q = dist * 2 + src_yh
                 both = jnp.concatenate(
@@ -317,31 +315,31 @@
     up_args = (back_up_out, up_send, up_recv, after, back_up_in)
     dn_args = (back_dn_out, dn_send, dn_recv, before, back_dn_in)
 
-    def use_up(place):
-        x = x_up[...]
+    def use_up(place, rows):
+        x = x_up[rows, :]
         gate = jnp.dot(x, wg[place], preferred_element_type=F32)
         upper = jnp.dot(x, wu[place], preferred_element_type=F32)
         middle = (jax.nn.silu(gate) * upper).astype(BF16)
 
         def add_up(step, _):
             at = pl.ds(pl.multiple_of(step * width, width), width)
-            acc_up[:, at] += jnp.dot(middle, wd[place, :, at], preferred_element_type=F32)
+            acc_up[rows, at] += jnp.dot(middle, wd[place, :, at], preferred_element_type=F32)
             return 0
 
         lax.fori_loop(0, features // width, add_up, 0)
 
-    def use_dn(place):
-        x = x_dn[...]
+    def use_dn(place, rows):
+        x = x_dn[rows, :]
         gate = jnp.dot(x, wg[place], preferred_element_type=F32)
         upper = jnp.dot(x, wu[place], preferred_element_type=F32)
-        pulled = contract_last(g_dn[...], wd[place])
+        pulled = contract_last(g_dn[rows, :], wd[place])
         sigma = jax.nn.sigmoid(gate)
         d_gate = (pulled * upper * sigma * (1.0 + gate * (1.0 - sigma))).astype(BF16)
         d_upper = (pulled * gate * sigma).astype(BF16)
 
         def add_dn(step, _):
             at = pl.ds(pl.multiple_of(step * width, width), width)
-            acc_dn[:, at] += contract_last(d_gate, wg[place, at, :]) + contract_last(d_upper, wu[place, at, :])
+            acc_dn[rows, at] += contract_last(d_gate, wg[place, at, :]) + contract_last(d_upper, wu[place, at, :])
             return 0
 
         lax.fori_loop(0, features // width, add_dn, 0)
@@ -349,9 +347,9 @@
     def at_step(step):
         return 2 * (step // 2) + 1 - leads_even + lax.rem(step, 2) * (2 * leads_even - 1)
 
-    def loop(use, first, end):
+    def loop(use, first, end, rows):
         def body(step, _):
-            use(at_step(step))
+            use(at_step(step), rows)
             return 0
 
         lax.fori_loop(first, end, body, 0)
@@ -367,15 +365,21 @@
     arrange(rows_up, x_up, None)
     for place in (lead_place(0), lead_place(1), follow_place(0)):
         wait_sibling(place)
-    loop(use_up, 0, 3)
+    part = n_src * CAP // 2
+    near, far = pl.ds(0, part), pl.ds(part, part)
+    loop(use_up, 0, 3, pl.ds(0, 2 * part))
     follow(1)
     wait_sibling(follow_place(1))
-    loop(use_up, 3, 4)
-    send_back(acc_up, *up_args)
+    loop(use_up, 3, 4, far)
+    send_back((3, 2), acc_up, *up_args)
+    loop(use_up, 3, 4, near)
+    send_back((1, 0), acc_up, *up_args)
     wait_rows(1)
     arrange(rows_dn, x_dn, g_dn)
-    loop(use_dn, 0, 4)
-    send_back(acc_dn, *dn_args)
+    loop(use_dn, 0, 4, far)
+    send_back((3, 2), acc_dn, *dn_args)
+    loop(use_dn, 0, 4, near)
+    send_back((1, 0), acc_dn, *dn_args)
 
     for copy in residuals:
         copy.wait_recv()
@@ -392,8 +396,8 @@
             ).wait_recv()
 
     wait_back(*up_args)
-    pick_up = unpick(meta_up_in[0:1, :])
-    gate_up_col = column(meta_up_in[1:2, :])
+    pick_up = unpick(route_up_in[...].astype(F32))
+    gate_up_col = column(weight_up_in[...])
 
     def finish_up(step, _):
         at = pl.ds(pl.multiple_of(step * width, width), width)
@@ -407,8 +411,8 @@
     lax.fori_loop(0, half // width, finish_up, 0)
 
     wait_back(*dn_args)
-    pick_dn = unpick(meta_dn_in[2:3, :])
-    gate_dn_col = column(meta_dn_in[3:4, :])
+    pick_dn = unpick(route_dn_in[...].astype(F32))
+    gate_dn_col = column(weight_dn_in[...])
 
     def pull_dn(step, carry):
         squares, dots = carry
@@ -470,23 +474,13 @@
     hidden = w_gate.shape[3]
     half = features // 2
     rows = EXPERTS * BLOCK
-    meta = jnp.concatenate(
-        [
-            routes_up.reshape(1, tokens).astype(F32),
-            gates_up.reshape(1, tokens),
-            routes_down.reshape(1, tokens).astype(F32),
-            gates_down.reshape(1, tokens),
-            jnp.zeros((4, tokens), F32),
-        ],
-        axis=0,
-    )
     vmem = pl.BlockSpec(memory_space=pltpu.VMEM)
     hbm = pl.BlockSpec(memory_space=pl.ANY)
     dma = pltpu.SemaphoreType.DMA
     up, down = pl.pallas_call(
         kernel,
         out_shape=(jax.ShapeDtypeStruct((tokens, features), BF16),) * 2,
-        in_specs=[vmem] * 5 + [hbm] * 3,
+        in_specs=[vmem] * 8 + [hbm] * 3,
         out_specs=(vmem, vmem),
         scratch_shapes=[
             pltpu.VMEM((SLICES, features, hidden), BF16),
@@ -511,8 +505,10 @@
             pltpu.VMEM((tokens, features), BF16),
             pltpu.VMEM((tokens, features), BF16),
             pltpu.VMEM((1, features), F32),
-            pltpu.VMEM((8, tokens), F32),
-            pltpu.VMEM((8, tokens), F32),
+            pltpu.VMEM((1, tokens), jnp.int32),
+            pltpu.VMEM((1, tokens), F32),
+            pltpu.VMEM((1, tokens), jnp.int32),
+            pltpu.VMEM((1, tokens), F32),
             dma((2, EXPERTS)),
             dma((2, EXPERTS)),
             dma((3, 2)),
@@ -523,15 +519,18 @@
             dma((EXPERTS,)),
             dma((EXPERTS,)),
             dma((EXPERTS,)),
-            dma((6,)),
-            dma((6,)),
+            dma((8,)),
+            dma((8,)),
         ],
         compiler_params=pltpu.CompilerParams(
             collective_id=0, has_side_effects=True, vmem_limit_bytes=60 * MIB
         ),
         cost_estimate=pl.CostEstimate(flops=12_000_000_000, bytes_accessed=12_000_000, transcendentals=400_000),
     )(
-        act_up[0], saved_down[0], grad_down[0], norm_gain, meta, w_gate[0, 0], w_up[0, 0], w_down[0, 0],
+        act_up[0], saved_down[0], grad_down[0], norm_gain,
+        routes_up.reshape(1, tokens), gates_up.reshape(1, tokens),
+        routes_down.reshape(1, tokens), gates_down.reshape(1, tokens),
+        w_gate[0, 0], w_up[0, 0], w_down[0, 0],
     )
     return up[None], down[None]
 

time: 314 us -> 310 us (0.987)
  no operation moved by 1% of the time
where the time goes in v4:
time: 310 us; the launch traced here: 306 us
  Pallas kernels  302 us (97%)
  local copies, waits for them, and re-layouts  3.17 us (1%)
    pallas_call x1, Pallas kernels, per_device(): pl.pallas_call(kernel, out_shape=(jax.ShapeDtypeStruct((tokens, features)...  302 us

profile of v4, /device:TPU:25, one launch (start us, length us, event | category | flops | bytes accessed | tf_op | source)
XLA Modules:
  0.0 305.8 jit_solution(1095261870334042394)
XLA Ops:
  0.6 302.0 %shard_map.122 = (bf16[128,3584]{1,0:T(8,128)(2,1)}, bf16[128,3584]{1,0:T(8,128)(2,1)}) custom-call(bf16[128,3584]{1,0:T(8,128)(2,1)} %bitcast.17, bf16[128,3584]{1,0:T(8,128)(2,1)} %bitcast.18, bf16[128,3584]{1,0:T(8,128)(2,1)} %bitcast.19, f32[1,3584]{1,0:T(1,128)} %gain.1, s32[1,128]{1,0:T(1,128)} %bitcast.20, f32[1,128]{1,0:T(1,128)} %bitcast.21, ...), custom_call_target="tpu_custom_call" | custom-call | flops 12000000000 | bytes 12000000 | tf_op jit(solution)/shard_map/pallas_call | solution.py:480
  302.6 0.0 copy-start
  302.6 2.2 copy.15
  304.9 0.0 copy-done
  304.9 0.9 copy.16
Async XLA Ops:
  302.6 2.3 copy-start

commit v5 on v4

--- a/solution.py
+++ b/solution.py
@@ -181,20 +181,33 @@
             row_block(packed, g), row_block(rows, slot), row_send.at[kind, g], row_recv.at[kind, slot], sec, peer
         )
 
-    def send_rows(kind):
+    def send_rows(kind, dists=(3, 2, 1, 0)):
         packed, rows = kinds[kind]
-        for g in range(EXPERTS):
-            peer, slot = host_of(g)
-
-            @pl.when(peer == me)
-            def _():
-                pltpu.make_async_copy(
-                    row_block(packed, g), row_block(rows, slot), row_recv.at[kind, slot]
-                ).start()
-
-            @pl.when(peer != me)
-            def _():
-                row_copy(kind, g)[1].start()
+        half_z, odd = z // 2, lax.rem(z, 2)
+        for dist in dists:
+            step = (0, 3, 1, 2)[dist] * (1 - odd) + (0, 1, 3, 2)[dist] * odd
+            to = lax.rem(half_z + step, 4)
+            for g_yh in range(2):
+                g = lax.rem(to, 2) * 4 + g_yh * 2 + to // 2
+                peer = (2 * to + nearest(lax.rem(z - 2 * to + 8, 8))[0]) * 4 + g_yh * 2 + c
+                slot = dist * 2 + yh
+                copy = remote(
+                    row_block(packed, g), row_block(rows, slot),
+                    row_send.at[kind, g], row_recv.at[kind, slot], sec, peer,
+                )
+                if dist:
+                    copy.start()
+                    continue
+
+                @pl.when(peer == me)
+                def _():
+                    pltpu.make_async_copy(
+                        row_block(packed, g), row_block(rows, slot), row_recv.at[kind, slot]
+                    ).start()
+
+                @pl.when(peer != me)
+                def _():
+                    copy.start()
 
     def wait_rows(kind):
         rows = kinds[kind][1]
@@ -355,14 +368,16 @@
         lax.fori_loop(first, end, body, 0)
 
     lead(0)
+    send_rows(1, (1, 0))
     lead(1)
-    send_rows(1)
+    send_rows(1, (3,))
     follow(0)
     for copy in residuals:
         copy.start()
 
     wait_rows(0)
     arrange(rows_up, x_up, None)
+    send_rows(1, (2,))
     for place in (lead_place(0), lead_place(1), follow_place(0)):
         wait_sibling(place)
     part = n_src * CAP // 2

time: 310 us -> 306 us (0.987); the launches traced: 306 us -> 306 us
  no operation moved by 1% of the time
where the time goes in v5:
time: 306 us
  Pallas kernels  302 us (99%)
  local copies, waits for them, and re-layouts  3.17 us (1%)
    pallas_call x1, Pallas kernels, per_device(): pl.pallas_call(kernel, out_shape=(jax.ShapeDtypeStruct((tokens, features)...  302 us

profile of v5, /device:TPU:25, one launch (start us, length us, event | category | flops | bytes accessed | tf_op | source)
XLA Modules:
  0.0 306.1 jit_solution(1187357295447278021)
XLA Ops:
  0.6 302.3 %shard_map.122 = (bf16[128,3584]{1,0:T(8,128)(2,1)}, bf16[128,3584]{1,0:T(8,128)(2,1)}) custom-call(bf16[128,3584]{1,0:T(8,128)(2,1)} %bitcast.17, bf16[128,3584]{1,0:T(8,128)(2,1)} %bitcast.18, bf16[128,3584]{1,0:T(8,128)(2,1)} %bitcast.19, f32[1,3584]{1,0:T(1,128)} %gain.1, s32[1,128]{1,0:T(1,128)} %bitcast.20, f32[1,128]{1,0:T(1,128)} %bitcast.21, ...), custom_call_target="tpu_custom_call" | custom-call | flops 12000000000 | bytes 12000000 | tf_op jit(solution)/shard_map/pallas_call | solution.py:495
  302.9 0.0 copy-start
  302.9 2.2 copy.15
  305.2 0.0 copy-done
  305.2 0.9 copy.16
Async XLA Ops:
  302.9 2.3 copy-start

commit v6 on v5

--- a/solution.py
+++ b/solution.py
@@ -370,8 +370,8 @@
     lead(0)
     send_rows(1, (1, 0))
     lead(1)
+    follow(0)
     send_rows(1, (3,))
-    follow(0)
     for copy in residuals:
         copy.start()
 

time: 306 us -> 306 us (level)
  no operation moved by 1% of the time
where the time goes in v6:
time: 306 us
  Pallas kernels  302 us (99%)
  local copies, waits for them, and re-layouts  3.17 us (1%)
    pallas_call x1, Pallas kernels, per_device(): pl.pallas_call(kernel, out_shape=(jax.ShapeDtypeStruct((tokens, features)...  302 us

profile of v6, /device:TPU:25, one launch (start us, length us, event | category | flops | bytes accessed | tf_op | source)
XLA Modules:
  0.0 306.1 jit_solution(16023566037476063416)
XLA Ops:
  0.6 302.3 %shard_map.122 = (bf16[128,3584]{1,0:T(8,128)(2,1)}, bf16[128,3584]{1,0:T(8,128)(2,1)}) custom-call(bf16[128,3584]{1,0:T(8,128)(2,1)} %bitcast.17, bf16[128,3584]{1,0:T(8,128)(2,1)} %bitcast.18, bf16[128,3584]{1,0:T(8,128)(2,1)} %bitcast.19, f32[1,3584]{1,0:T(1,128)} %gain.1, s32[1,128]{1,0:T(1,128)} %bitcast.20, f32[1,128]{1,0:T(1,128)} %bitcast.21, ...), custom_call_target="tpu_custom_call" | custom-call | flops 12000000000 | bytes 12000000 | tf_op jit(solution)/shard_map/pallas_call | solution.py:495
  302.9 0.0 copy-start
  302.9 2.2 copy.15
  305.2 0.0 copy-done
  305.2 0.9 copy.16
Async XLA Ops:
  302.9 2.3 copy-start
